TPU v7x, 32 devices: a whole 2x2x4 slice. The times are simulated.
32 devices in a mesh: dp: 8 (over y, x, core), tensor: 4 (over z).
Axes of the slice: x: 2, y: 2, z: 4, core: 2. Of those that a mesh axis runs over, the one named last changes fastest.
Arguments:
- block_input: bfloat16 [8192, 1536], P(('dp', 'tensor')), may hold values from -6 to 6
- attn_gain: bfloat16 [1536], P('dp'), may hold values from 0.5 to 1.5
- w_query: bfloat16 [1536, 1536], P('dp', 'tensor'), may hold values from -0.15625 to 0.15625
- w_key: bfloat16 [1536, 1536], P('dp', 'tensor'), may hold values from -0.15625 to 0.15625
- w_value: bfloat16 [1536, 1536], P('dp', 'tensor'), may hold values from -0.15625 to 0.15625
- w_forget: bfloat16 [1536, 24], P(None, 'tensor'), may hold values from -0.15625 to 0.15625
- forget_bias: float32 [24], P('tensor'), may hold values from -1 to 7
- w_output: bfloat16 [1536, 1536], P('tensor', 'dp'), may hold values from -0.625 to 0.625
- mlp_gain: bfloat16 [1536], P('dp'), may hold values from 0.5 to 1.5
- w_gate: bfloat16 [1536, 4096], P('dp', 'tensor'), may hold values from -0.15625 to 0.15625
- w_up: bfloat16 [1536, 4096], P('dp', 'tensor'), may hold values from -0.15625 to 0.15625
- w_down: bfloat16 [4096, 1536], P('tensor', 'dp'), may hold values from -0.09375 to 0.09375
- segment_ids: int32 [8, 1024], P('dp'), may hold values from 0 to 3, never falling along the last dimension, each value on 1 to 512 neighbouring positions
- cotangent: bfloat16 [8192, 1536], P(('dp', 'tensor')), may hold values from -6 to 6
Outputs:
- output: bfloat16 [8192, 1536], P(('dp', 'tensor'))
- input_grad: float32 [8192, 1536], P(('dp', 'tensor'))
- grad_attn_gain: float32 [1536], P('dp')
- grad_w_query: float32 [1536, 1536], P('dp', 'tensor')
- grad_w_key: float32 [1536, 1536], P('dp', 'tensor')
- grad_w_value: float32 [1536, 1536], P('dp', 'tensor')
- grad_w_forget: float32 [1536, 24], P(None, 'tensor')
- grad_forget_bias: float32 [24], P('tensor')
- grad_w_output: float32 [1536, 1536], P('tensor', 'dp')
- grad_mlp_gain: float32 [1536], P('dp')
- grad_w_gate: float32 [1536, 4096], P('dp', 'tensor')
- grad_w_up: float32 [1536, 4096], P('dp', 'tensor')
- grad_w_down: float32 [4096, 1536], P('tensor', 'dp')
Inputs may be any that keep to these rules, and one draw needn't show every extreme that they name: Each row of segment_ids numbers the documents of one sequence in order, never falling; a document has 1 to 512 tokens, and the longest of a row has exactly 512.
All inputs are finite; a program needn't handle non-finite values.
Results may differ from a plain program's by a relative error of at most 0.018.
Values may be sent and summed in bfloat16 or wider, within the bound.
No kernel may reach another device: no remote copies, remote signals or barrier semaphores. Data moves between devices by JAX's collectives and lax.ppermute only.
A program may use at most 128 MiB of HBM per device.

v0:
```python
from functools import reduce
import jax
import jax.numpy as jnp
from jax import lax
from jax.sharding import PartitionSpec as P

HEAD_DIM = 64
EPS = 1e-06


def norm_rows(value, gain):
    scale = lax.rsqrt(jnp.mean(value * value, axis=-1, keepdims=True) + EPS)
    return (value * scale * gain, scale)


def norm_back(value, scale, gain, grad):
    weighted = grad * gain
    inner = jnp.mean(weighted * value, axis=-1, keepdims=True)
    return scale * weighted - value * (scale * scale * scale) * inner


def right_product(left, right):
    return jnp.dot(left, right, preferred_element_type=jnp.float32)


def back_terms(pairs):
    terms = [
        jnp.einsum("se,de->sd", grad, weight, preferred_element_type=jnp.float32)
        for grad, weight in pairs
    ]
    return reduce(jnp.add, terms)


def pair_scores(query_pair, key_pair, cum_pair, seg_row, start, block):
    length = key_pair.shape[0]
    raw = jnp.einsum("qhd,khd->hqk", query_pair, key_pair, preferred_element_type=jnp.float32)
    cum_rows = lax.dynamic_slice_in_dim(cum_pair, start, block, 1)
    scores = raw * 0.125 + cum_rows[:, :, None] - cum_pair[:, None, :]
    positions = start + jnp.arange(block, dtype=jnp.int32)
    columns = jnp.arange(length, dtype=jnp.int32)
    seg_rows = lax.dynamic_slice_in_dim(seg_row, start, block, 0)
    allowed = (columns[None, :] <= positions[:, None]) & (seg_rows[:, None] == seg_row[None, :])
    return jnp.where(allowed[None], scores, -jnp.inf)


def pair_inputs(index, blocks, block, query, keys, values, cumul):
    length = query.shape[0]
    span = 2 * HEAD_DIM
    group = index // blocks
    start = index % blocks * block
    column = group * span
    query_pair = lax.dynamic_slice(query, (start, column), (block, span)).reshape(
        block, 2, HEAD_DIM
    )
    key_pair = lax.dynamic_slice_in_dim(keys, column, span, 1).reshape(length, 2, HEAD_DIM)
    value_pair = lax.dynamic_slice_in_dim(values, column, span, 1).reshape(length, 2, HEAD_DIM)
    cum_pair = lax.dynamic_slice_in_dim(cumul, group * 2, 2, 0)
    return (group, start, column, query_pair, key_pair, value_pair, cum_pair)


def attend(query, keys, values, cumul, seg_row):
    length = query.shape[0]
    heads = query.shape[1] // HEAD_DIM
    block = min(512, length)
    blocks = length // block
    span = 2 * HEAD_DIM

    def step(index, carry):
        mixed, log_total = carry
        group, start, column, query_pair, key_pair, value_pair, cum_pair = pair_inputs(
            index, blocks, block, query, keys, values, cumul
        )
        scores = pair_scores(query_pair, key_pair, cum_pair, seg_row, start, block)
        top = jnp.max(scores, axis=-1, keepdims=True)
        expd = jnp.exp(scores - top)
        total = jnp.sum(expd, axis=-1, keepdims=True)
        probs = (expd / total).astype(jnp.bfloat16)
        out = jnp.einsum("hqk,khd->qhd", probs, value_pair, preferred_element_type=jnp.float32)
        mixed = lax.dynamic_update_slice(
            mixed, out.astype(jnp.bfloat16).reshape(block, span), (start, column)
        )
        log_total = lax.dynamic_update_slice(
            log_total, (top + jnp.log(total))[:, :, 0], (group * 2, start)
        )
        return (mixed, log_total)

    start_state = (jnp.zeros_like(query), jnp.zeros((heads, length), jnp.float32))
    return lax.fori_loop(0, heads // 2 * blocks, step, start_state)


def attend_back(query, keys, values, cumul, seg_row, log_total, grad_mixed):
    length = query.shape[0]
    heads = query.shape[1] // HEAD_DIM
    block = min(512, length)
    blocks = length // block
    span = 2 * HEAD_DIM

    def step(index, carry):
        grad_query, grad_keys, grad_values, grad_cum = carry
        group, start, column, query_pair, key_pair, value_pair, cum_pair = pair_inputs(
            index, blocks, block, query, keys, values, cumul
        )
        grad_pair = lax.dynamic_slice(grad_mixed, (start, column), (block, span)).reshape(
            block, 2, HEAD_DIM
        )
        scores = pair_scores(query_pair, key_pair, cum_pair, seg_row, start, block)
        lse_rows = lax.dynamic_slice(log_total, (group * 2, start), (2, block))
        probs = jnp.exp(scores - lse_rows[:, :, None])
        grad_probs = jnp.einsum(
            "qhd,khd->hqk", grad_pair, value_pair, preferred_element_type=jnp.float32
        )
        inner = jnp.sum(probs * grad_probs, axis=-1, keepdims=True)
        grad_scores = probs * (grad_probs - inner)
        rounded = grad_scores.astype(jnp.bfloat16)
        part_query = (
            jnp.einsum("hqk,khd->qhd", rounded, key_pair, preferred_element_type=jnp.float32)
            * 0.125
        )
        part_keys = (
            jnp.einsum("hqk,qhd->khd", rounded, query_pair, preferred_element_type=jnp.float32)
            * 0.125
        )
        part_values = jnp.einsum(
            "hqk,qhd->khd",
            probs.astype(jnp.bfloat16),
            grad_pair,
            preferred_element_type=jnp.float32,
        )
        grad_query = lax.dynamic_update_slice(
            grad_query, part_query.reshape(block, span), (start, column)
        )
        strip_keys = lax.dynamic_slice_in_dim(grad_keys, column, span, 1) + part_keys.reshape(
            length, span
        )
        grad_keys = lax.dynamic_update_slice_in_dim(grad_keys, strip_keys, column, 1)
        strip_values = lax.dynamic_slice_in_dim(grad_values, column, span, 1) + part_values.reshape(
            length, span
        )
        grad_values = lax.dynamic_update_slice_in_dim(grad_values, strip_values, column, 1)
        cum_cols = lax.dynamic_slice_in_dim(grad_cum, group * 2, 2, 0) - jnp.sum(
            grad_scores, axis=1
        )
        grad_cum = lax.dynamic_update_slice_in_dim(grad_cum, cum_cols, group * 2, 0)
        cum_rows = lax.dynamic_slice(grad_cum, (group * 2, start), (2, block)) + jnp.sum(
            grad_scores, axis=-1
        )
        grad_cum = lax.dynamic_update_slice(grad_cum, cum_rows, (group * 2, start))
        return (grad_query, grad_keys, grad_values, grad_cum)

    zeros_wide = jnp.zeros(query.shape, jnp.float32)
    start_state = (zeros_wide, zeros_wide, zeros_wide, jnp.zeros((heads, length), jnp.float32))
    return lax.fori_loop(0, heads // 2 * blocks, step, start_state)


def per_device(
    block_input,
    attn_gain,
    w_query,
    w_key,
    w_value,
    w_forget,
    forget_bias,
    w_output,
    mlp_gain,
    w_gate,
    w_up,
    w_down,
    segment_ids,
    cotangent,
):
    width = block_input.shape[1]
    heads = w_forget.shape[1]
    query_full, key_full, value_full, output_full, gain_one = (
        lax.all_gather(w_query, "dp", axis=0, tiled=True),
        lax.all_gather(w_key, "dp", axis=0, tiled=True),
        lax.all_gather(w_value, "dp", axis=0, tiled=True),
        lax.all_gather(w_output, "dp", axis=1, tiled=True),
        lax.all_gather(attn_gain, "dp", axis=0, tiled=True),
    )
    gate_full, up_full, down_full, gain_two = (
        lax.all_gather(w_gate, "dp", axis=0, tiled=True),
        lax.all_gather(w_up, "dp", axis=0, tiled=True),
        lax.all_gather(w_down, "dp", axis=1, tiled=True),
        lax.all_gather(mlp_gain, "dp", axis=0, tiled=True),
    )
    resid = block_input.astype(jnp.float32)
    normed, first_scale = norm_rows(resid, gain_one.astype(jnp.float32))
    normed_all = lax.all_gather(normed.astype(jnp.bfloat16), "tensor", axis=0, tiled=True)
    query = jnp.dot(normed_all, query_full, preferred_element_type=jnp.float32).astype(jnp.bfloat16)
    keys = jnp.dot(normed_all, key_full, preferred_element_type=jnp.float32).astype(jnp.bfloat16)
    values = jnp.dot(normed_all, value_full, preferred_element_type=jnp.float32).astype(
        jnp.bfloat16
    )
    forget_logit = jnp.dot(normed_all, w_forget, preferred_element_type=jnp.float32) + forget_bias
    cumul = jnp.cumsum(jax.nn.log_sigmoid(forget_logit), axis=0).T
    seg_row = segment_ids[0]
    mixed, log_total = attend(query, keys, values, cumul, seg_row)
    attn_out = lax.psum_scatter(
        right_product(mixed, output_full), "tensor", scatter_dimension=0, tiled=True
    )
    hidden_res = resid + attn_out
    second, second_scale = norm_rows(hidden_res, gain_two.astype(jnp.float32))
    second_all = lax.all_gather(second.astype(jnp.bfloat16), "tensor", axis=0, tiled=True)
    gate = jnp.dot(second_all, gate_full, preferred_element_type=jnp.float32)
    upper = jnp.dot(second_all, up_full, preferred_element_type=jnp.float32)
    sigma = jax.nn.sigmoid(gate)
    swish = gate * sigma
    hidden = (swish * upper).astype(jnp.bfloat16)
    mlp_out = lax.psum_scatter(
        right_product(hidden, down_full).astype(jnp.bfloat16),
        "tensor",
        scatter_dimension=0,
        tiled=True,
    ).astype(jnp.float32)
    output = (hidden_res + mlp_out).astype(jnp.bfloat16)
    (
        query_full,
        key_full,
        value_full,
        output_full,
        gain_one,
        gate_full,
        up_full,
        down_full,
        gain_two,
    ) = (
        lax.all_gather(w_query, "dp", axis=0, tiled=True),
        lax.all_gather(w_key, "dp", axis=0, tiled=True),
        lax.all_gather(w_value, "dp", axis=0, tiled=True),
        lax.all_gather(w_output, "dp", axis=1, tiled=True),
        lax.all_gather(attn_gain, "dp", axis=0, tiled=True),
        lax.all_gather(w_gate, "dp", axis=0, tiled=True),
        lax.all_gather(w_up, "dp", axis=0, tiled=True),
        lax.all_gather(w_down, "dp", axis=1, tiled=True),
        lax.all_gather(mlp_gain, "dp", axis=0, tiled=True),
    )
    grad_out = cotangent.astype(jnp.float32)
    grad_all = lax.all_gather(cotangent, "tensor", axis=0, tiled=True)
    grad_hidden = (
        jnp.einsum("sd,fd->sf", grad_all, down_full, preferred_element_type=jnp.float32)
        .astype(jnp.bfloat16)
        .astype(jnp.float32)
    )
    grad_gate = (grad_hidden * upper * sigma * (1.0 + gate * (1.0 - sigma))).astype(jnp.bfloat16)
    grad_up = (grad_hidden * swish).astype(jnp.bfloat16)
    grad_down_w = jnp.einsum("sf,sd->fd", hidden, grad_all, preferred_element_type=jnp.float32)
    grad_gate_w = jnp.einsum("sd,sf->df", second_all, grad_gate, preferred_element_type=jnp.float32)
    grad_up_w = jnp.einsum("sd,sf->df", second_all, grad_up, preferred_element_type=jnp.float32)
    grad_second = lax.psum_scatter(
        back_terms(((grad_gate, gate_full), (grad_up, up_full))).astype(jnp.bfloat16),
        "tensor",
        scatter_dimension=0,
        tiled=True,
    ).astype(jnp.float32)
    gain_two_f = gain_two.astype(jnp.float32)
    grad_res = grad_out + norm_back(hidden_res, second_scale, gain_two_f, grad_second)
    gain_two_part = jnp.sum(grad_second * hidden_res * second_scale, axis=0)
    mlp_shards = (
        lax.psum_scatter(
            grad_gate_w.astype(jnp.bfloat16), "dp", scatter_dimension=0, tiled=True
        ).astype(jnp.float32),
        lax.psum_scatter(
            grad_up_w.astype(jnp.bfloat16), "dp", scatter_dimension=0, tiled=True
        ).astype(jnp.float32),
        lax.psum_scatter(
            grad_down_w.astype(jnp.bfloat16), "dp", scatter_dimension=1, tiled=True
        ).astype(jnp.float32),
    )
    grad_branch = grad_res.astype(jnp.bfloat16)
    branch_all = lax.all_gather(grad_branch, "tensor", axis=0, tiled=True)
    grad_mixed = jnp.einsum(
        "sd,ed->se", branch_all, output_full, preferred_element_type=jnp.float32
    ).astype(jnp.bfloat16)
    grad_output_w = jnp.einsum("se,sd->ed", mixed, branch_all, preferred_element_type=jnp.float32)
    grad_query, grad_keys, grad_values, grad_cum = attend_back(
        query, keys, values, cumul, seg_row, log_total, grad_mixed
    )
    grad_logf = jnp.flip(jnp.cumsum(jnp.flip(grad_cum.T, 0), axis=0), 0)
    grad_logit = grad_logf * jax.nn.sigmoid(-forget_logit)
    grad_bias = jnp.sum(grad_logit, axis=0)
    logit_low = grad_logit.astype(jnp.bfloat16)
    query_low = grad_query.astype(jnp.bfloat16)
    keys_low = grad_keys.astype(jnp.bfloat16)
    values_low = grad_values.astype(jnp.bfloat16)
    grad_query_w = jnp.einsum(
        "sd,se->de", normed_all, query_low, preferred_element_type=jnp.float32
    )
    grad_key_w = jnp.einsum("sd,se->de", normed_all, keys_low, preferred_element_type=jnp.float32)
    grad_value_w = jnp.einsum(
        "sd,se->de", normed_all, values_low, preferred_element_type=jnp.float32
    )
    grad_forget_w = jnp.einsum(
        "sd,sh->dh", normed_all, logit_low, preferred_element_type=jnp.float32
    )
    grad_first = lax.psum_scatter(
        back_terms(
            (
                (query_low, query_full),
                (keys_low, key_full),
                (values_low, value_full),
                (logit_low, w_forget),
            )
        ).astype(jnp.bfloat16),
        "tensor",
        scatter_dimension=0,
        tiled=True,
    ).astype(jnp.float32)
    gain_one_f = gain_one.astype(jnp.float32)
    input_grad = grad_res + norm_back(resid, first_scale, gain_one_f, grad_first)
    gain_one_part = jnp.sum(grad_first * resid * first_scale, axis=0)
    attn_shards = (
        lax.psum_scatter(
            grad_query_w.astype(jnp.bfloat16), "dp", scatter_dimension=0, tiled=True
        ).astype(jnp.float32),
        lax.psum_scatter(
            grad_key_w.astype(jnp.bfloat16), "dp", scatter_dimension=0, tiled=True
        ).astype(jnp.float32),
        lax.psum_scatter(
            grad_value_w.astype(jnp.bfloat16), "dp", scatter_dimension=0, tiled=True
        ).astype(jnp.float32),
        lax.psum_scatter(
            grad_output_w.astype(jnp.bfloat16), "dp", scatter_dimension=1, tiled=True
        ).astype(jnp.float32),
    )
    tensor_index = lax.axis_index("tensor")
    all_heads = heads * lax.axis_size("tensor")
    forget_pad = lax.dynamic_update_slice(
        jnp.zeros((width, all_heads), jnp.float32), grad_forget_w, (0, tensor_index * heads)
    )
    bias_pad = lax.dynamic_update_slice(
        jnp.zeros((all_heads,), jnp.float32), grad_bias, (tensor_index * heads,)
    )
    summed = lax.psum((forget_pad, bias_pad, gain_one_part, gain_two_part), ("dp", "tensor"))
    share = width // lax.axis_size("dp")
    dp_start = lax.axis_index("dp") * share
    grad_forget_out = lax.dynamic_slice_in_dim(summed[0], tensor_index * heads, heads, 1)
    grad_bias_out = lax.dynamic_slice_in_dim(summed[1], tensor_index * heads, heads, 0)
    grad_gain_one = lax.dynamic_slice_in_dim(summed[2], dp_start, share, 0)
    grad_gain_two = lax.dynamic_slice_in_dim(summed[3], dp_start, share, 0)
    return (
        output,
        input_grad,
        grad_gain_one,
        attn_shards[0],
        attn_shards[1],
        attn_shards[2],
        grad_forget_out,
        grad_bias_out,
        attn_shards[3],
        grad_gain_two,
        mlp_shards[0],
        mlp_shards[1],
        mlp_shards[2],
    )


def solution(mesh):
    return jax.shard_map(
        per_device,
        mesh=mesh,
        in_specs=(
            P(("dp", "tensor"), None),
            P("dp"),
            P("dp", "tensor"),
            P("dp", "tensor"),
            P("dp", "tensor"),
            P(None, "tensor"),
            P("tensor"),
            P("tensor", "dp"),
            P("dp"),
            P("dp", "tensor"),
            P("dp", "tensor"),
            P("tensor", "dp"),
            P("dp", None),
            P(("dp", "tensor"), None),
        ),
        out_specs=(
            P(("dp", "tensor"), None),
            P(("dp", "tensor"), None),
            P("dp"),
            P("dp", "tensor"),
            P("dp", "tensor"),
            P("dp", "tensor"),
            P(None, "tensor"),
            P("tensor"),
            P("tensor", "dp"),
            P("dp"),
            P("dp", "tensor"),
            P("dp", "tensor"),
            P("tensor", "dp"),
        ),
        check_vma=False,
    )
```

profile of v0, /device:TPU:0, one launch (start us, length us, event | category | flops | bytes accessed | tf_op | source)
XLA Modules:
  0.0 1310.2 jit_solution(17133466086450550335)
XLA Ops:
  12.8 15.4 %all-reduce.3 = (bf16[1536]{0:T(1024)(128)(2,1)S(1)}, bf16[1536]{0:T(1024)(128)(2,1)S(1)}) all-reduce(bf16[1536]{0:T(1024)(128)(2,1)S(1)} %dynamic-update-slice, bf16[1536]{0:T(1024)(128)(2,1)S(1)} %dynamic-update-slice.1), channel_id=1, replica_groups=mesh['dp'=8,'tensor'=4] {'dp'}, use_global_device_ids=true, to_apply=%add | all-reduce | flops 3072 | bytes 12288
  28.9 2.3 fusion.29
  33.9 60.3 %all-gather.12.cloned.1.call-done = bf16[1024,1536]{1,0:T(8,128)(2,1)} async-done(((bf16[256,1536]{1,0:T(8,128)(2,1)}), bf16[1024,1536]{1,0:T(8,128)(2,1)}) %all-gather.12.cloned.1.call-update) | async-done | bytes 3145744 | tf_op jit(solution)/shard_map/all_gather | solution.py:188
  94.2 2.9 convolution_add_fusion
  99.9 18.9 %all-gather.18.cloned.1.call-done = bf16[1536,384]{1,0:T(8,128)(2,1)} async-done(((bf16[192,384]{1,0:T(8,128)(2,1)}), bf16[1536,384]{1,0:T(8,128)(2,1)}) %all-gather.18.cloned.1.call-update) | async-done | bytes 1179664 | tf_op jit(solution)/shard_map/all_gather | solution.py:175
  118.8 3.9 convolution_convert_fusion.10
  122.8 2.3 copy.36
  125.0 19.8 %all-gather.16.cloned.1.call-done = bf16[1536,384]{1,0:T(8,128)(2,1)} async-done(((bf16[192,384]{1,0:T(8,128)(2,1)}), bf16[1536,384]{1,0:T(8,128)(2,1)}) %all-gather.16.cloned.1.call-update) | async-done | bytes 1179664 | tf_op jit(solution)/shard_map/all_gather | solution.py:174
  144.8 3.9 convolution_convert_fusion.11
  148.7 2.3 copy.35
  151.0 19.6 %all-gather.14.cloned.1.call-done = bf16[1536,384]{1,0:T(8,128)(2,1)} async-done(((bf16[192,384]{1,0:T(8,128)(2,1)}), bf16[1536,384]{1,0:T(8,128)(2,1)}) %all-gather.14.cloned.1.call-update) | async-done | bytes 1179664 | tf_op jit(solution)/shard_map/all_gather | solution.py:176
  170.6 3.9 convolution_convert_fusion.12
  176.1 59.4 %while.40 = (s32[]{:T(128)}, bf16[1024,384]{0,1:T(8,128)(2,1)S(1)}, f32[6,1024]{1,0:T(8,128)S(1)}, bf16[1024,384]{0,1:T(8,128)(2,1)S(1)}, s32[1024]{0:T(1024)S(1...) while((s32[]{:T(128)}, bf16[1024,384]{0,1:T(8,128)(2,1)S(1)}, ...), condition=%wide.region_6.7_spmd, body=%wide.region_3.6_spmd.sunk | while | flops 288947744 | bytes 17148404 | solution.py:88
  183.9 2.8 dynamic_update_slice.97
  204.1 2.8 dynamic_update_slice.97
  235.5 6.3 fusion.58
  244.4 108.4 %reduce-scatter.12.cloned.1.call-done = f32[256,1536]{1,0:T(8,128)} async-done(((f32[1024,1536]{1,0:T(8,128)}), f32[256,1536]{1,0:T(8,128)}) %reduce-scatter.12.cloned.1.call-update) | async-done | bytes 1572880 | tf_op jit(solution)/shard_map/reduce_scatter | solution.py:198
  356.4 62.0 %all-gather.30.cloned.1.call-done = bf16[1024,1536]{1,0:T(8,128)(2,1)} async-done(((bf16[256,1536]{1,0:T(8,128)(2,1)}), bf16[1024,1536]{1,0:T(8,128)(2,1)}) %all-gather.30.cloned.1.call-update) | async-done | bytes 3145744 | tf_op jit(solution)/shard_map/all_gather | solution.py:238
  418.4 32.9 %all-gather.28.cloned.1.call-done = bf16[1024,1536]{0,1:T(8,128)(2,1)} async-done(((bf16[1024,192]{0,1:T(8,128)(2,1)}), bf16[1024,1536]{0,1:T(8,128)(2,1)}) %all-gather.28.cloned.1.call-update) | async-done | bytes 3145744 | tf_op jit(solution)/shard_map/all_gather | solution.py:183
  451.3 7.6 convolution_convert_fusion.8
  458.9 26.6 %all-gather.24.cloned.1.call-done = bf16[1536,1024]{1,0:T(8,128)(2,1)} async-done(((bf16[192,1024]{1,0:T(8,128)(2,1)}), bf16[1536,1024]{1,0:T(8,128)(2,1)}) %all-gather.24.cloned.1.call-update) | async-done | bytes 3145744 | tf_op jit(solution)/shard_map/all_gather | solution.py:181
  485.5 65.5 %all-gather.22.cloned.1.call-done = bf16[1024,1536]{1,0:T(8,128)(2,1)} async-done(((bf16[256,1536]{1,0:T(8,128)(2,1)}), bf16[1024,1536]{1,0:T(8,128)(2,1)}) %all-gather.22.cloned.1.call-update) | async-done | bytes 3145744 | tf_op jit(solution)/shard_map/all_gather | solution.py:203
  551.1 8.2 fusion.59
  559.3 24.7 %all-gather.26.cloned.1.call-done = bf16[1536,1024]{1,0:T(8,128)(2,1)} async-done(((bf16[192,1024]{1,0:T(8,128)(2,1)}), bf16[1536,1024]{1,0:T(8,128)(2,1)}) %all-gather.26.cloned.1.call-update) | async-done | bytes 3145744 | tf_op jit(solution)/shard_map/all_gather | solution.py:182
  583.9 10.9 fusion.14
  594.8 3.5 fusion.60
  599.3 6.8 add_convert_fusion.1
  606.2 60.4 %reduce-scatter.16.cloned.1.call-done = bf16[256,1536]{1,0:T(8,128)(2,1)} async-done(((bf16[1024,1536]{1,0:T(8,128)(2,1)}), bf16[256,1536]{1,0:T(8,128)(2,1)}) %reduce-scatter.16.cloned.1.call-update) | async-done | bytes 786448 | tf_op jit(solution)/shard_map/reduce_scatter | solution.py:249
  666.5 2.2 fusion.26
  668.8 2.6 fusion.52
  671.4 9.0 convolution_convert_fusion.1
  680.5 7.7 convolution_convert_fusion.2
  689.4 7.7 convolution_convert_fusion
  697.2 37.8 %all-gather.32.cloned.1.call-done = bf16[1024,1536]{1,0:T(8,128)(2,1)} async-done(((bf16[256,1536]{1,0:T(8,128)(2,1)}), bf16[1024,1536]{1,0:T(8,128)(2,1)}) %all-gather.32.cloned.1.call-update) | async-done | bytes 3145744 | tf_op jit(solution)/shard_map/all_gather | solution.py:270
  735.0 4.5 convolution_convert_fusion.9
  741.1 91.9 %while.41 = (s32[]{:T(128)}, bf16[1024,384]{0,1:T(8,128)(2,1)}, f32[1024,384]{0,1:T(8,128)}, f32[1024,384]{0,1:T(8,128)S(1)}, f32[6,1024]{1,0:T(8,128)S(1)}, /*i...) while((s32[]{:T(128)}, bf16[1024,384]{0,1:T(8,128)(2,1)}, ...), condition=%wide.region_16.17_spmd, body=%wide.region_12.16_spmd.sunk | while | flops 686816768 | bytes 53156532 | solution.py:152
  747.2 2.0 multiply_reduce_fusion.3
  752.3 3.4 dynamic_update_slice.101
  768.3 2.8 dynamic_update_slice.101
  778.5 2.0 multiply_reduce_fusion.3
  783.6 3.4 dynamic_update_slice.101
  799.6 2.8 dynamic_update_slice.101
  809.8 2.0 multiply_reduce_fusion.3
  814.9 2.1 dynamic_update_slice.101
  824.5 2.0 multiply_reduce_fusion.3
  836.4 2.4 fusion.49
  840.2 5.2 convolution_convert_fusion.4
  845.5 5.3 convolution_convert_fusion.7
  850.8 5.2 convolution_convert_fusion.6
  856.1 4.8 convolution_convert_fusion.5
  861.2 3.4 fusion.61
  868.5 2.9 add_convert_fusion
  871.4 7.7 convolution_convert_fusion.3
  879.2 2.0 convert_element_type.210
  881.3 2.0 convert_element_type.208
  885.5 124.8 %all-reduce.6.cloned.1.call-done = f32[1536,24]{0,1:T(8,128)} async-done(((f32[1536,24]{0,1:T(8,128)}), f32[1536,24]{0,1:T(8,128)}) %all-reduce.6.cloned.1.call-update) | async-done | bytes 147472 | tf_op jit(solution)/shard_map/psum | solution.py:333
  1011.8 40.7 %reduce-scatter.26.cloned.1.call-done = bf16[384,192]{0,1:T(8,128)(2,1)} async-done(((bf16[384,1536]{0,1:T(8,128)(2,1)}), bf16[384,192]{0,1:T(8,128)(2,1)}) %reduce-scatter.26.cloned.1.call-update) | async-done | bytes 147472 | tf_op jit(solution)/shard_map/reduce_scatter | solution.py:321
  1054.1 38.4 %reduce-scatter.20.cloned.1.call-done = bf16[192,384]{1,0:T(8,128)(2,1)} async-done(((bf16[1536,384]{1,0:T(8,128)(2,1)}), bf16[192,384]{1,0:T(8,128)(2,1)}) %reduce-scatter.20.cloned.1.call-update) | async-done | bytes 147472 | tf_op jit(solution)/shard_map/reduce_scatter | solution.py:312
  1094.1 38.6 %reduce-scatter.22.cloned.1.call-done = bf16[192,384]{1,0:T(8,128)(2,1)} async-done(((bf16[1536,384]{1,0:T(8,128)(2,1)}), bf16[192,384]{1,0:T(8,128)(2,1)}) %reduce-scatter.22.cloned.1.call-update) | async-done | bytes 147472 | tf_op jit(solution)/shard_map/reduce_scatter | solution.py:315
  1134.3 38.4 %reduce-scatter.24.cloned.1.call-done = bf16[192,384]{1,0:T(8,128)(2,1)} async-done(((bf16[1536,384]{1,0:T(8,128)(2,1)}), bf16[192,384]{1,0:T(8,128)(2,1)}) %reduce-scatter.24.cloned.1.call-update) | async-done | bytes 147472 | tf_op jit(solution)/shard_map/reduce_scatter | solution.py:318
  1174.4 61.0 %reduce-scatter.18.cloned.1.call-done = bf16[256,1536]{1,0:T(8,128)(2,1)} async-done(((bf16[1024,1536]{1,0:T(8,128)(2,1)}), bf16[256,1536]{1,0:T(8,128)(2,1)}) %reduce-scatter.18.cloned.1.call-update) | async-done | bytes 786448 | tf_op jit(solution)/shard_map/reduce_scatter | solution.py:295
  1237.1 45.5 %all-reduce.2 = (f32[1536]{0:T(1024)S(1)}, f32[24]{0:T(128)S(1)}, f32[1536]{0:T(1024)S(1)}) all-reduce(f32[1536]{0:T(1024)S(1)} %get-tuple-element.679, f32[24]{0:T(128)S(1)} %dynamic_update_slice.84, f32[1536]{0:T(1024)S(1)} %copy-done.25), channel_id=1, replica_groups=mesh['dp'=8,'tensor'=4] {'dp','tensor'}, use_global_device_ids=true, to_apply=%region_22.23 | all-reduce | flops 3096 | bytes 24768 | tf_op jit(solution)/shard_map/psum | solution.py:333
  1284.4 14.7 %reduce-scatter.14.cloned.1.call-done = bf16[256,1536]{1,0:T(8,128)(2,1)} async-done(((bf16[1024,1536]{1,0:T(8,128)(2,1)}), bf16[256,1536]{1,0:T(8,128)(2,1)}) %reduce-scatter.14.cloned.1.call-update) | async-done | bytes 786448 | tf_op jit(solution)/shard_map/reduce_scatter | solution.py:209
  1299.2 4.0 fusion.21
  (422 shorter events, 167.2 us)
Async XLA Ops:
  7.2 87.0 %copy-start = (bf16[1536,6]{0,1:T(8,128)(2,1)S(1)}, bf16[1536,6]{0,1:T(8,128)(2,1)}, u32[]{:S(2)}) copy-start(bf16[1536,6]{0,1:T(8,128)(2,1)} %param.23) | copy-start | bytes 55300
  7.2 87.0 %copy-start.35 = (f32[6]{0:T(128)S(1)}, f32[6]{0:T(128)}, u32[]{:S(2)}) copy-start(f32[6]{0:T(128)} %param.24) | copy-start | bytes 76
  7.2 87.0 %all-gather.12.cloned.1.call-start = ((), (), s32[]{:S(2)}) async-start(), calls=%async_computation.11 | async-start | bytes 3932160 | tf_op jit(solution)/shard_map/all_gather | solution.py:188
  9.2 24.6 %copy-start.28 = (f32[256]{0:T(256)}, f32[256]{0:T(256)S(1)}, u32[]{:S(2)}) copy-start(f32[256]{0:T(256)S(1)} %get-tuple-element.748) | copy-start | bytes 3076
  31.2 87.7 %all-gather.18.cloned.1.call-start = ((), (), s32[]{:S(2)}) async-start(), calls=%async_computation.14 | async-start | bytes 1327104 | tf_op jit(solution)/shard_map/all_gather | solution.py:175
  31.9 112.9 %all-gather.16.cloned.1.call-start = ((), (), s32[]{:S(2)}) async-start(), calls=%async_computation.13 | async-start | bytes 1327104 | tf_op jit(solution)/shard_map/all_gather | solution.py:174
  32.7 138.0 %all-gather.14.cloned.1.call-start = ((), (), s32[]{:S(2)}) async-start(), calls=%async_computation.12 | async-start | bytes 1327104 | tf_op jit(solution)/shard_map/all_gather | solution.py:176
  33.2 202.3 %all-gather.20.cloned.1.call-start = ((), (), s32[]{:S(2)}) async-start(), calls=%async_computation.15 | async-start | bytes 1327104 | tf_op jit(solution)/shard_map/all_gather | solution.py:177
  33.8 318.9 %reduce-scatter.12.cloned.1.call-start = ((), (), s32[]{:S(2)}) async-start(), calls=%async_computation.16 | async-start | bytes 7864320 | tf_op jit(solution)/shard_map/reduce_scatter | solution.py:198
  94.2 24.6 %copy-start.1 = (bf16[1024,1536]{1,0:T(8,128)(2,1)S(1)}, bf16[1024,1536]{1,0:T(8,128)(2,1)}, u32[]{:S(2)}) copy-start(bf16[1024,1536]{1,0:T(8,128)(2,1)} %all-gather.12.cloned.1.call-done) | copy-start | bytes 9437188
  151.0 25.1 %copy-start.14 = (s32[1,1024]{1,0:T(1,128)S(1)}, s32[1,1024]{1,0:T(1,128)}, u32[]{:S(2)}) copy-start(s32[1,1024]{1,0:T(1,128)} %param.30) | copy-start | bytes 12292
  235.5 6.3 copy-start.7
  235.5 6.3 copy-start.10
  241.8 110.9 %copy-start.5 = (bf16[256,1536]{1,0:T(8,128)(2,1)S(1)}, bf16[256,1536]{1,0:T(8,128)(2,1)}, u32[]{:S(2)}) copy-start(bf16[256,1536]{1,0:T(8,128)(2,1)} %param.18) | copy-start | bytes 2359300
  241.9 176.5 %all-gather.30.cloned.1.call-start = ((), (), s32[]{:S(2)}) async-start(), calls=%async_computation.22 | async-start | bytes 3932160 | tf_op jit(solution)/shard_map/all_gather | solution.py:238
  242.6 208.7 %all-gather.28.cloned.1.call-start = ((), (), s32[]{:S(2)}) async-start(), calls=%async_computation.20 | async-start | bytes 3538944 | tf_op jit(solution)/shard_map/all_gather | solution.py:183
  243.4 242.2 %all-gather.24.cloned.1.call-start = ((), (), s32[]{:S(2)}) async-start(), calls=%async_computation.18 | async-start | bytes 3538944 | tf_op jit(solution)/shard_map/all_gather | solution.py:181
  244.1 306.9 %all-gather.22.cloned.1.call-start = ((), (), s32[]{:S(2)}) async-start(), calls=%async_computation.17 | async-start | bytes 3932160 | tf_op jit(solution)/shard_map/all_gather | solution.py:203
  244.4 424.4 %copy-start.18 = (f32[1536]{0:T(1024)}, f32[1536]{0:T(1024)S(1)}, u32[]{:S(2)}) copy-start(f32[1536]{0:T(1024)S(1)} %convert_element_type.178) | copy-start | bytes 18436
  354.5 314.2 %copy-start.26 = (f32[256]{0:T(256)}, f32[256]{0:T(256)S(1)}, u32[]{:S(2)}) copy-start(f32[256]{0:T(256)S(1)} %get-tuple-element.750) | copy-start | bytes 3076
  354.5 314.2 %copy-start.30 = (f32[256]{0:T(256)}, f32[256]{0:T(256)S(1)}, u32[]{:S(2)}) copy-start(f32[256]{0:T(256)S(1)} %get-tuple-element.749) | copy-start | bytes 3076
  355.6 228.3 %all-gather.26.cloned.1.call-start = ((), (), s32[]{:S(2)}) async-start(), calls=%async_computation.19 | async-start | bytes 3538944 | tf_op jit(solution)/shard_map/all_gather | solution.py:182
  356.4 310.2 %reduce-scatter.16.cloned.1.call-start = ((), (), s32[]{:S(2)}) async-start(), calls=%async_computation.23 | async-start | bytes 3932160 | tf_op jit(solution)/shard_map/reduce_scatter | solution.py:249
  583.9 10.9 copy-start.36
  594.8 3.6 copy-start.39
  594.8 3.6 copy-start.37
  594.8 3.9 copy-start.38
  594.8 4.5 copy-start.40
  606.1 62.6 %copy-start.8 = (bf16[256,1536]{1,0:T(8,128)(2,1)S(1)}, bf16[256,1536]{1,0:T(8,128)(2,1)}, u32[]{:S(2)}) copy-start(bf16[256,1536]{1,0:T(8,128)(2,1)} %param.31) | copy-start | bytes 2359300
  606.1 128.9 %all-gather.32.cloned.1.call-start = ((), (), s32[]{:S(2)}) async-start(), calls=%async_computation.24 | async-start | bytes 3932160 | tf_op jit(solution)/shard_map/all_gather | solution.py:270
  668.7 11.7 copy-start.32
  671.3 207.8 %reduce-scatter.30.cloned.1.call-start = ((), (), s32[]{:S(2)}) async-start(), calls=%async_computation.32 | async-start | bytes 3538944 | tf_op jit(solution)/shard_map/reduce_scatter | solution.py:262
  680.4 200.9 %reduce-scatter.28.cloned.1.call-start = ((), (), s32[]{:S(2)}) async-start(), calls=%async_computation.31 | async-start | bytes 3538944 | tf_op jit(solution)/shard_map/reduce_scatter | solution.py:259
  688.2 195.1 %reduce-scatter.32.cloned.1.call-start = ((), (), s32[]{:S(2)}) async-start(), calls=%async_computation.33 | async-start | bytes 3538944 | tf_op jit(solution)/shard_map/reduce_scatter | solution.py:265
  697.1 37.9 %copy-start.13 = (bf16[384,1536]{0,1:T(8,128)(2,1)S(1)}, bf16[384,1536]{0,1:T(8,128)(2,1)}, u32[]{:S(2)}) copy-start(bf16[384,1536]{0,1:T(8,128)(2,1)} %all-gather.20.cloned.1.call-done) | copy-start | bytes 3538948
  697.2 313.1 %all-reduce.6.cloned.1.call-start = ((), (), s32[]{:S(2)}) async-start(), calls=%async_computation.29 | async-start | bytes 294912 | tf_op jit(solution)/shard_map/psum | solution.py:333
  741.1 95.2 %copy-start.17 = (f32[1024,6]{0,1:T(8,128)S(1)}, f32[1024,6]{0,1:T(8,128)}, u32[]{:S(2)}) copy-start(f32[1024,6]{0,1:T(8,128)} %copy-done.16) | copy-start | bytes 73732
  750.9 4.8 copy-start.2
  751.7 5.4 copy-start.24
  766.9 4.2 copy-start.2
  767.6 4.8 copy-start.24
  782.2 4.8 copy-start.2
  783.0 5.4 copy-start.24
  798.2 4.2 copy-start.2
  799.0 4.8 copy-start.24
  813.5 3.5 copy-start.2
  814.3 4.2 copy-start.24
  829.0 4.0 copy-start.24
  839.9 212.6 %reduce-scatter.26.cloned.1.call-start = ((), (), s32[]{:S(2)}) async-start(), calls=%async_computation.30 | async-start | bytes 1327104 | tf_op jit(solution)/shard_map/reduce_scatter | solution.py:321
  845.4 247.1 %reduce-scatter.20.cloned.1.call-start = ((), (), s32[]{:S(2)}) async-start(), calls=%async_computation.26 | async-start | bytes 1327104 | tf_op jit(solution)/shard_map/reduce_scatter | solution.py:312
  850.8 281.9 %reduce-scatter.22.cloned.1.call-start = ((), (), s32[]{:S(2)}) async-start(), calls=%async_computation.27 | async-start | bytes 1327104 | tf_op jit(solution)/shard_map/reduce_scatter | solution.py:315
  856.1 316.7 %reduce-scatter.24.cloned.1.call-start = ((), (), s32[]{:S(2)}) async-start(), calls=%async_computation.28 | async-start | bytes 1327104 | tf_op jit(solution)/shard_map/reduce_scatter | solution.py:318
  860.9 374.5 %reduce-scatter.18.cloned.1.call-start = ((), (), s32[]{:S(2)}) async-start(), calls=%async_computation.25 | async-start | bytes 3932160 | tf_op jit(solution)/shard_map/reduce_scatter | solution.py:295
  871.4 427.8 %reduce-scatter.14.cloned.1.call-start = ((), (), s32[]{:S(2)}) async-start(), calls=%async_computation.21 | async-start | bytes 3932160 | tf_op jit(solution)/shard_map/reduce_scatter | solution.py:209
  879.1 356.3 %copy-start.6 = (bf16[256,1536]{1,0:T(8,128)(2,1)S(1)}, bf16[256,1536]{1,0:T(8,128)(2,1)}, u32[]{:S(2)}) copy-start(bf16[256,1536]{1,0:T(8,128)(2,1)} %param.18) | copy-start | bytes 2359300
  879.1 356.3 %copy-start.21 = (f32[1536]{0:T(1024)S(1)}, f32[1536]{0:T(1024)}, u32[]{:S(2)}) copy-start(f32[1536]{0:T(1024)} %copy-done.20) | copy-start | bytes 18436
  879.1 356.3 %copy-start.29 = (f32[256]{0:T(256)S(1)}, f32[256]{0:T(256)}, u32[]{:S(2)}) copy-start(f32[256]{0:T(256)} %copy-done.28) | copy-start | bytes 3076
  881.2 355.8 %copy-start.25 = (f32[1536]{0:T(1024)S(1)}, f32[1536]{0:T(1024)}, u32[]{:S(2)}) copy-start(f32[1536]{0:T(1024)} %get-tuple-element.677) | copy-start | bytes 18436
  881.2 418.0 %copy-start.9 = (bf16[256,1536]{1,0:T(8,128)(2,1)S(1)}, bf16[256,1536]{1,0:T(8,128)(2,1)}, u32[]{:S(2)}) copy-start(bf16[256,1536]{1,0:T(8,128)(2,1)} %param.31) | copy-start | bytes 2359300
  881.2 418.0 %copy-start.19 = (f32[1536]{0:T(1024)S(1)}, f32[1536]{0:T(1024)}, u32[]{:S(2)}) copy-start(f32[1536]{0:T(1024)} %copy-done.18) | copy-start | bytes 18436
  881.2 418.0 %copy-start.27 = (f32[256]{0:T(256)S(1)}, f32[256]{0:T(256)}, u32[]{:S(2)}) copy-start(f32[256]{0:T(256)} %copy-done.26) | copy-start | bytes 3076
  881.2 418.0 %copy-start.31 = (f32[256]{0:T(256)S(1)}, f32[256]{0:T(256)}, u32[]{:S(2)}) copy-start(f32[256]{0:T(256)} %copy-done.30) | copy-start | bytes 3076
  881.2 418.0 %copy-start.33 = (f32[256]{0:T(256)S(1)}, f32[256]{0:T(256)}, u32[]{:S(2)}) copy-start(f32[256]{0:T(256)} %copy-done.32) | copy-start | bytes 3076
  881.2 418.0 %copy-start.34 = (f32[256]{0:T(256)S(1)}, f32[256]{0:T(256)}, u32[]{:S(2)}) copy-start(f32[256]{0:T(256)} %get-tuple-element.747) | copy-start | bytes 3076
  (25 other events, 43.9 us)
Sparse Core Ops, SparseCore 0:
  31.3 62.8 all-gather.11
  96.1 22.6 all-gather.17
  120.7 24.0 all-gather.15
  146.5 24.0 all-gather.13
  172.4 24.0 all-gather.19
  242.0 110.7 reduce-scatter.11
  354.3 64.0 all-gather.29
  420.3 30.9 all-gather.27
  453.2 32.3 all-gather.23
  487.5 63.4 all-gather.21
  552.9 30.9 all-gather.25
  606.3 60.2 reduce-scatter.15
  671.5 63.5 all-gather.31
  738.3 44.9 reduce-scatter.29
  786.8 46.2 reduce-scatter.27
  836.3 46.3 reduce-scatter.31
  889.6 120.6 all-reduce.5
  1013.7 38.7 reduce-scatter.25
  1055.7 36.7 reduce-scatter.19
  1095.9 36.7 reduce-scatter.21
  1135.9 36.7 reduce-scatter.23
  1175.2 60.2 reduce-scatter.17
  1237.9 61.3 reduce-scatter.13
where the time goes:
time: 1320 us; the launch traced here: 1310 us
  waiting for transfers between devices  899 us (68%)
  matrix products  175 us (13%)
  local copies, waits for them, and re-layouts  96.2 us (7%)
  blocking collectives  61 us (5%)
  other arithmetic  60.4 us (5%)
  between operations  15.6 us (1%)
    psum x1, waiting for transfers between devices, per_device(): lax.psum((forget_pad, bias_pad, gain_one_part, gain_two_part), ('dp', 'te...  125 us
    reduce_scatter x1, waiting for transfers between devices, per_device(): lax.psum_scatter(right_product(mixed, output_full), 'tensor', scatter_dim...  108 us
    all_gather x1, waiting for transfers between devices, per_device(): lax.all_gather(second.astype(jnp.bfloat16), 'tensor', axis=0, tiled=True)  65.5 us
    all_gather x1, waiting for transfers between devices, per_device(): grad_all = lax.all_gather(cotangent, 'tensor', axis=0, tiled=True)  62 us
    reduce_scatter x1, waiting for transfers between devices, per_device(): lax.psum_scatter(back_terms(((query_low, query_full), (keys_low, key_full...  61 us
    reduce_scatter x1, waiting for transfers between devices, per_device(): lax.psum_scatter(back_terms(((grad_gate, gate_full), (grad_up, up_full)))...  60.4 us
    all_gather x1, waiting for transfers between devices, per_device(): lax.all_gather(normed.astype(jnp.bfloat16), 'tensor', axis=0, tiled=True)  60.3 us
    psum x1, blocking collectives, per_device(): lax.psum((forget_pad, bias_pad, gain_one_part, gain_two_part), ('dp', 'te...  45.5 us
  transfers between devices with their start and end apart: 23, of which 19 were waited for; matrix products, arithmetic and copies ran while one was open for 21% of the time, Pallas kernels for 0%

commit v1 on v0

--- a/solution.py
+++ b/solution.py
@@ -330,7 +330,13 @@
     bias_pad = lax.dynamic_update_slice(
         jnp.zeros((all_heads,), jnp.float32), grad_bias, (tensor_index * heads,)
     )
-    summed = lax.psum((forget_pad, bias_pad, gain_one_part, gain_two_part), ("dp", "tensor"))
+
+    def pair_rounds(m, axis_key, group_axis):
+        for dev in (axis_key, group_axis):
+            m = lax.psum(m, dev)
+        return m
+
+    summed = pair_rounds((forget_pad, bias_pad, gain_one_part, gain_two_part), "tensor", "dp")
     share = width // lax.axis_size("dp")
     dp_start = lax.axis_index("dp") * share
     grad_forget_out = lax.dynamic_slice_in_dim(summed[0], tensor_index * heads, heads, 1)

time: 1320 us -> 1380 us (1.045)
  waiting for transfers between devices: 899 us -> 972 us
    psum x1 -> x2, waiting for transfers between devices: 125 us -> 61.1 us  [pair_rounds(): m = lax.psum(m, dev)]
    reduce_scatter x1, waiting for transfers between devices: 0.01 us -> 47.9 us  [per_device(): lax.psum_scatter(grad_down_w.astype(jnp.bfloat16), 'dp', scatter_dimensio...]
    reduce_scatter x1, waiting for transfers between devices: 0.02 us -> 47.5 us  [per_device(): lax.psum_scatter(grad_gate_w.astype(jnp.bfloat16), 'dp', scatter_dimensio...]
    all_gather x1, waiting for transfers between devices: 37.8 us -> 62.6 us  [per_device(): branch_all = lax.all_gather(grad_branch, 'tensor', axis=0, tiled=True)]
    psum x1 -> x2, blocking collectives: 45.5 us -> 41.7 us  [pair_rounds(): m = lax.psum(m, dev)]
  transfers between devices with their start and end apart: 23 -> 24, of which waited for: 19 -> 23; matrix products, arithmetic and copies ran while one was open for 21% -> 12% of each run, Pallas kernels for 0% -> 0%
where the time goes in v1:
time: 1380 us; the launch traced here: 1370 us
  waiting for transfers between devices  972 us (70%)
  matrix products  176 us (13%)
  local copies, waits for them, and re-layouts  83.3 us (6%)
  other arithmetic  60.4 us (4%)
  blocking collectives  57.1 us (4%)
  between operations  16 us (1%)
    reduce_scatter x1, waiting for transfers between devices, per_device(): lax.psum_scatter(right_product(mixed, output_full), 'tensor', scatter_dim...  108 us
    all_gather x1, waiting for transfers between devices, per_device(): lax.all_gather(second.astype(jnp.bfloat16), 'tensor', axis=0, tiled=True)  65.5 us
    all_gather x1, waiting for transfers between devices, per_device(): branch_all = lax.all_gather(grad_branch, 'tensor', axis=0, tiled=True)  62.6 us
    all_gather x1, waiting for transfers between devices, per_device(): grad_all = lax.all_gather(cotangent, 'tensor', axis=0, tiled=True)  62 us
    psum x2, waiting for transfers between devices, pair_rounds(): m = lax.psum(m, dev)  61.1 us
    reduce_scatter x1, waiting for transfers between devices, per_device(): lax.psum_scatter(back_terms(((query_low, query_full), (keys_low, key_full...  61 us
    reduce_scatter x1, waiting for transfers between devices, per_device(): lax.psum_scatter(back_terms(((grad_gate, gate_full), (grad_up, up_full)))...  60.4 us
    all_gather x1, waiting for transfers between devices, per_device(): lax.all_gather(normed.astype(jnp.bfloat16), 'tensor', axis=0, tiled=True)  60.3 us
  transfers between devices with their start and end apart: 24, of which 23 were waited for; matrix products, arithmetic and copies ran while one was open for 12% of the time, Pallas kernels for 0%

profile of v1, /device:TPU:0, one launch (start us, length us, event | category | flops | bytes accessed | tf_op | source)
XLA Modules:
  0.0 1367.8 jit_solution(2650914501283626880)
XLA Ops:
  12.8 15.4 %all-reduce.4 = (bf16[1536]{0:T(1024)(128)(2,1)S(1)}, bf16[1536]{0:T(1024)(128)(2,1)S(1)}) all-reduce(bf16[1536]{0:T(1024)(128)(2,1)S(1)} %dynamic-update-slice, bf16[1536]{0:T(1024)(128)(2,1)S(1)} %dynamic-update-slice.1), channel_id=1, replica_groups=mesh['dp'=8,'tensor'=4] {'dp'}, use_global_device_ids=true, to_apply=%add | all-reduce | flops 3072 | bytes 12288
  28.3 2.3 fusion.29
  33.3 60.3 %all-gather.12.cloned.1.call-done = bf16[1024,1536]{1,0:T(8,128)(2,1)} async-done(((bf16[256,1536]{1,0:T(8,128)(2,1)}), bf16[1024,1536]{1,0:T(8,128)(2,1)}) %all-gather.12.cloned.1.call-update) | async-done | bytes 3145744 | tf_op jit(solution)/shard_map/all_gather | solution.py:188
  93.6 2.8 convolution_add_fusion
  98.6 19.6 %all-gather.18.cloned.1.call-done = bf16[1536,384]{1,0:T(8,128)(2,1)} async-done(((bf16[192,384]{1,0:T(8,128)(2,1)}), bf16[1536,384]{1,0:T(8,128)(2,1)}) %all-gather.18.cloned.1.call-update) | async-done | bytes 1179664 | tf_op jit(solution)/shard_map/all_gather | solution.py:175
  118.2 4.0 convolution_convert_fusion.10
  122.6 21.7 %all-gather.16.cloned.1.call-done = bf16[1536,384]{1,0:T(8,128)(2,1)} async-done(((bf16[192,384]{1,0:T(8,128)(2,1)}), bf16[1536,384]{1,0:T(8,128)(2,1)}) %all-gather.16.cloned.1.call-update) | async-done | bytes 1179664 | tf_op jit(solution)/shard_map/all_gather | solution.py:174
  144.2 4.0 convolution_convert_fusion.11
  148.5 21.5 %all-gather.14.cloned.1.call-done = bf16[1536,384]{1,0:T(8,128)(2,1)} async-done(((bf16[192,384]{1,0:T(8,128)(2,1)}), bf16[1536,384]{1,0:T(8,128)(2,1)}) %all-gather.14.cloned.1.call-update) | async-done | bytes 1179664 | tf_op jit(solution)/shard_map/all_gather | solution.py:176
  170.1 4.0 convolution_convert_fusion.12
  175.4 51.8 %while.40 = (s32[]{:T(128)}, bf16[1024,384]{0,1:T(8,128)(2,1)}, f32[6,1024]{1,0:T(8,128)S(1)}, bf16[1024,384]{0,1:T(8,128)(2,1)S(1)}, s32[1024]{0:T(1024)S(1)}, ...) while((s32[]{:T(128)}, bf16[1024,384]{0,1:T(8,128)(2,1)}, ...), condition=%wide.region_6.7_spmd, body=%wide.region_3.6_spmd.sunk | while | flops 288947744 | bytes 17148404 | solution.py:88
  181.2 3.4 dynamic_update_slice.97
  190.5 2.8 dynamic_update_slice.97
  199.2 3.4 dynamic_update_slice.97
  208.4 2.8 dynamic_update_slice.97
  217.1 2.1 dynamic_update_slice.97
  227.3 6.8 fusion.58
  236.6 108.4 %reduce-scatter.12.cloned.1.call-done = f32[256,1536]{1,0:T(8,128)} async-done(((f32[1024,1536]{1,0:T(8,128)}), f32[256,1536]{1,0:T(8,128)}) %reduce-scatter.12.cloned.1.call-update) | async-done | bytes 1572880 | tf_op jit(solution)/shard_map/reduce_scatter | solution.py:198
  348.6 62.0 %all-gather.30.cloned.1.call-done = bf16[1024,1536]{1,0:T(8,128)(2,1)} async-done(((bf16[256,1536]{1,0:T(8,128)(2,1)}), bf16[1024,1536]{1,0:T(8,128)(2,1)}) %all-gather.30.cloned.1.call-update) | async-done | bytes 3145744 | tf_op jit(solution)/shard_map/all_gather | solution.py:238
  410.6 32.9 %all-gather.28.cloned.1.call-done = bf16[1024,1536]{0,1:T(8,128)(2,1)} async-done(((bf16[1024,192]{0,1:T(8,128)(2,1)}), bf16[1024,1536]{0,1:T(8,128)(2,1)}) %all-gather.28.cloned.1.call-update) | async-done | bytes 3145744 | tf_op jit(solution)/shard_map/all_gather | solution.py:183
  443.5 7.6 convolution_convert_fusion.8
  451.1 26.6 %all-gather.24.cloned.1.call-done = bf16[1536,1024]{1,0:T(8,128)(2,1)} async-done(((bf16[192,1024]{1,0:T(8,128)(2,1)}), bf16[1536,1024]{1,0:T(8,128)(2,1)}) %all-gather.24.cloned.1.call-update) | async-done | bytes 3145744 | tf_op jit(solution)/shard_map/all_gather | solution.py:181
  477.8 65.5 %all-gather.22.cloned.1.call-done = bf16[1024,1536]{1,0:T(8,128)(2,1)} async-done(((bf16[256,1536]{1,0:T(8,128)(2,1)}), bf16[1024,1536]{1,0:T(8,128)(2,1)}) %all-gather.22.cloned.1.call-update) | async-done | bytes 3145744 | tf_op jit(solution)/shard_map/all_gather | solution.py:203
  543.3 8.2 fusion.59
  551.5 24.7 %all-gather.26.cloned.1.call-done = bf16[1536,1024]{1,0:T(8,128)(2,1)} async-done(((bf16[192,1024]{1,0:T(8,128)(2,1)}), bf16[1536,1024]{1,0:T(8,128)(2,1)}) %all-gather.26.cloned.1.call-update) | async-done | bytes 3145744 | tf_op jit(solution)/shard_map/all_gather | solution.py:182
  576.2 10.9 fusion.14
  587.1 3.5 fusion.60
  591.6 6.8 add_convert_fusion.1
  598.5 60.4 %reduce-scatter.16.cloned.1.call-done = bf16[256,1536]{1,0:T(8,128)(2,1)} async-done(((bf16[1024,1536]{1,0:T(8,128)(2,1)}), bf16[256,1536]{1,0:T(8,128)(2,1)}) %reduce-scatter.16.cloned.1.call-update) | async-done | bytes 786448 | tf_op jit(solution)/shard_map/reduce_scatter | solution.py:249
  658.8 2.2 fusion.26
  661.1 2.6 fusion.52
  664.7 62.6 %all-gather.32.cloned.1.call-done = bf16[1024,1536]{1,0:T(8,128)(2,1)} async-done(((bf16[256,1536]{1,0:T(8,128)(2,1)}), bf16[1024,1536]{1,0:T(8,128)(2,1)}) %all-gather.32.cloned.1.call-update) | async-done | bytes 3145744 | tf_op jit(solution)/shard_map/all_gather | solution.py:270
  727.3 4.9 convolution_convert_fusion.9
  733.7 91.7 %while.41 = (s32[]{:T(128)}, bf16[1024,384]{0,1:T(8,128)(2,1)}, f32[1024,384]{0,1:T(8,128)}, f32[1024,384]{0,1:T(8,128)S(1)}, f32[6,1024]{1,0:T(8,128)S(1)}, /*i...) while((s32[]{:T(128)}, bf16[1024,384]{0,1:T(8,128)(2,1)}, ...), condition=%wide.region_16.17_spmd, body=%wide.region_12.16_spmd.sunk | while | flops 686816768 | bytes 53156532 | solution.py:152
  744.9 3.4 dynamic_update_slice.101
  760.8 2.8 dynamic_update_slice.101
  776.1 3.4 dynamic_update_slice.101
  792.0 2.8 dynamic_update_slice.101
  807.4 2.1 dynamic_update_slice.101
  828.8 2.4 fusion.49
  832.6 9.0 convolution_convert_fusion.1
  841.6 7.7 convolution_convert_fusion.2
  849.4 7.7 convolution_convert_fusion
  857.1 8.4 all-reduce.8.cloned.1.call-done
  865.7 5.0 convolution_convert_fusion.4
  870.8 5.0 convolution_convert_fusion.7
  875.9 5.6 convolution_convert_fusion.6
  881.6 4.9 convolution_convert_fusion.5
  886.8 3.4 fusion.61
  894.1 2.9 add_convert_fusion
  897.1 7.8 convolution_convert_fusion.3
  904.9 10.4 reduce-scatter.30.cloned.1.call-done
  917.3 47.5 %reduce-scatter.28.cloned.1.call-done = bf16[192,1024]{1,0:T(8,128)(2,1)} async-done(((bf16[1536,1024]{1,0:T(8,128)(2,1)}), bf16[192,1024]{1,0:T(8,128)(2,1)}) %reduce-scatter.28.cloned.1.call-update) | async-done | bytes 393232 | tf_op jit(solution)/shard_map/reduce_scatter | solution.py:259
  966.8 47.9 %reduce-scatter.32.cloned.1.call-done = bf16[1024,192]{0,1:T(8,128)(2,1)} async-done(((bf16[1024,1536]{0,1:T(8,128)(2,1)}), bf16[1024,192]{0,1:T(8,128)(2,1)}) %reduce-scatter.32.cloned.1.call-update) | async-done | bytes 393232 | tf_op jit(solution)/shard_map/reduce_scatter | solution.py:265
  1016.9 52.8 %all-reduce.10.cloned.1.call-done = f32[1536,24]{0,1:T(8,128)} async-done(((f32[1536,24]{0,1:T(8,128)}), f32[1536,24]{0,1:T(8,128)}) %all-reduce.10.cloned.1.call-update) | async-done | bytes 147472 | tf_op jit(solution)/shard_map/psum | solution.py:336
  1071.1 39.3 %reduce-scatter.26.cloned.1.call-done = bf16[384,192]{0,1:T(8,128)(2,1)} async-done(((bf16[384,1536]{0,1:T(8,128)(2,1)}), bf16[384,192]{0,1:T(8,128)(2,1)}) %reduce-scatter.26.cloned.1.call-update) | async-done | bytes 147472 | tf_op jit(solution)/shard_map/reduce_scatter | solution.py:321
  1112.1 38.6 %reduce-scatter.20.cloned.1.call-done = bf16[192,384]{1,0:T(8,128)(2,1)} async-done(((bf16[1536,384]{1,0:T(8,128)(2,1)}), bf16[192,384]{1,0:T(8,128)(2,1)}) %reduce-scatter.20.cloned.1.call-update) | async-done | bytes 147472 | tf_op jit(solution)/shard_map/reduce_scatter | solution.py:312
  1152.3 38.4 %reduce-scatter.22.cloned.1.call-done = bf16[192,384]{1,0:T(8,128)(2,1)} async-done(((bf16[1536,384]{1,0:T(8,128)(2,1)}), bf16[192,384]{1,0:T(8,128)(2,1)}) %reduce-scatter.22.cloned.1.call-update) | async-done | bytes 147472 | tf_op jit(solution)/shard_map/reduce_scatter | solution.py:315
  1192.3 38.7 %reduce-scatter.24.cloned.1.call-done = bf16[192,384]{1,0:T(8,128)(2,1)} async-done(((bf16[1536,384]{1,0:T(8,128)(2,1)}), bf16[192,384]{1,0:T(8,128)(2,1)}) %reduce-scatter.24.cloned.1.call-update) | async-done | bytes 147472 | tf_op jit(solution)/shard_map/reduce_scatter | solution.py:318
  1232.7 61.0 %reduce-scatter.18.cloned.1.call-done = bf16[256,1536]{1,0:T(8,128)(2,1)} async-done(((bf16[1024,1536]{1,0:T(8,128)(2,1)}), bf16[256,1536]{1,0:T(8,128)(2,1)}) %reduce-scatter.18.cloned.1.call-update) | async-done | bytes 786448 | tf_op jit(solution)/shard_map/reduce_scatter | solution.py:295
  1295.3 18.3 %all-reduce.3 = (f32[1536]{0:T(1024)S(1)}, f32[24]{0:T(128)S(1)}, f32[1536]{0:T(1024)S(1)}) all-reduce(f32[1536]{0:T(1024)S(1)} %get-tuple-element.679, f32[24]{0:T(128)S(1)} %dynamic_update_slice.84, f32[1536]{0:T(1024)S(1)} %copy-done.24), channel_id=1, replica_groups=mesh['dp'=8,'tensor'=4] {'tensor'}, use_global_device_ids=true, to_apply=%region_22.23 | all-reduce | flops 3096 | bytes 24768 | tf_op jit(solution)/shard_map/psum | solution.py:336
  1313.6 23.4 %all-reduce.2 = (f32[1536]{0:T(1024)S(1)}, f32[24]{0:T(128)S(1)}, f32[1536]{0:T(1024)S(1)}) all-reduce(f32[1536]{0:T(1024)S(1)} %get-tuple-element.728, f32[24]{0:T(128)S(1)} %get-tuple-element.729, f32[1536]{0:T(1024)S(1)} %get-tuple-element.730), channel_id=1, replica_groups=mesh['dp'=8,'tensor'=4] {'dp'}, use_global_device_ids=true, to_apply=%region_23.24 | all-reduce | flops 3096 | bytes 24768 | tf_op jit(solution)/shard_map/psum | solution.py:336
  1338.8 17.6 %reduce-scatter.14.cloned.1.call-done = bf16[256,1536]{1,0:T(8,128)(2,1)} async-done(((bf16[1024,1536]{1,0:T(8,128)(2,1)}), bf16[256,1536]{1,0:T(8,128)(2,1)}) %reduce-scatter.14.cloned.1.call-update) | async-done | bytes 786448 | tf_op jit(solution)/shard_map/reduce_scatter | solution.py:209
  1356.5 4.0 fusion.21
  (424 shorter events, 162.1 us)
Async XLA Ops:
  7.2 86.4 %copy-start = (bf16[1536,6]{0,1:T(8,128)(2,1)S(1)}, bf16[1536,6]{0,1:T(8,128)(2,1)}, u32[]{:S(2)}) copy-start(bf16[1536,6]{0,1:T(8,128)(2,1)} %param.23) | copy-start | bytes 55300
  7.2 86.4 %copy-start.34 = (f32[6]{0:T(128)S(1)}, f32[6]{0:T(128)}, u32[]{:S(2)}) copy-start(f32[6]{0:T(128)} %param.24) | copy-start | bytes 76
  7.2 86.4 %all-gather.12.cloned.1.call-start = ((), (), s32[]{:S(2)}) async-start(), calls=%async_computation.11 | async-start | bytes 3932160 | tf_op jit(solution)/shard_map/all_gather | solution.py:188
  9.2 24.1 %copy-start.27 = (f32[256]{0:T(256)}, f32[256]{0:T(256)S(1)}, u32[]{:S(2)}) copy-start(f32[256]{0:T(256)S(1)} %get-tuple-element.751) | copy-start | bytes 3076
  28.3 5.0 copy-start.19
  30.6 87.7 %all-gather.18.cloned.1.call-start = ((), (), s32[]{:S(2)}) async-start(), calls=%async_computation.14 | async-start | bytes 1327104 | tf_op jit(solution)/shard_map/all_gather | solution.py:175
  31.3 112.9 %all-gather.16.cloned.1.call-start = ((), (), s32[]{:S(2)}) async-start(), calls=%async_computation.13 | async-start | bytes 1327104 | tf_op jit(solution)/shard_map/all_gather | solution.py:174
  32.1 138.0 %all-gather.14.cloned.1.call-start = ((), (), s32[]{:S(2)}) async-start(), calls=%async_computation.12 | async-start | bytes 1327104 | tf_op jit(solution)/shard_map/all_gather | solution.py:176
  32.7 194.6 %all-gather.20.cloned.1.call-start = ((), (), s32[]{:S(2)}) async-start(), calls=%async_computation.15 | async-start | bytes 1327104 | tf_op jit(solution)/shard_map/all_gather | solution.py:177
  33.2 311.8 %reduce-scatter.12.cloned.1.call-start = ((), (), s32[]{:S(2)}) async-start(), calls=%async_computation.16 | async-start | bytes 7864320 | tf_op jit(solution)/shard_map/reduce_scatter | solution.py:198
  96.4 21.8 %copy-start.15 = (f32[1024,6]{0,1:T(8,128)}, f32[1024,6]{0,1:T(8,128)S(1)}, u32[]{:S(2)}) copy-start(f32[1024,6]{0,1:T(8,128)S(1)} %convolution_add_fusion) | copy-start | bytes 73732
  148.5 26.8 %copy-start.13 = (s32[1,1024]{1,0:T(1,128)S(1)}, s32[1,1024]{1,0:T(1,128)}, u32[]{:S(2)}) copy-start(s32[1,1024]{1,0:T(1,128)} %param.30) | copy-start | bytes 12292
  227.2 6.9 copy-start.6
  227.2 6.9 copy-start.7
  227.2 6.9 copy-start.10
  234.1 110.9 %copy-start.4 = (bf16[256,1536]{1,0:T(8,128)(2,1)S(1)}, bf16[256,1536]{1,0:T(8,128)(2,1)}, u32[]{:S(2)}) copy-start(bf16[256,1536]{1,0:T(8,128)(2,1)} %param.18) | copy-start | bytes 2359300
  234.1 176.5 %all-gather.30.cloned.1.call-start = ((), (), s32[]{:S(2)}) async-start(), calls=%async_computation.22 | async-start | bytes 3932160 | tf_op jit(solution)/shard_map/all_gather | solution.py:238
  234.9 208.7 %all-gather.28.cloned.1.call-start = ((), (), s32[]{:S(2)}) async-start(), calls=%async_computation.20 | async-start | bytes 3538944 | tf_op jit(solution)/shard_map/all_gather | solution.py:183
  235.6 242.2 %all-gather.24.cloned.1.call-start = ((), (), s32[]{:S(2)}) async-start(), calls=%async_computation.18 | async-start | bytes 3538944 | tf_op jit(solution)/shard_map/all_gather | solution.py:181
  236.3 306.9 %all-gather.22.cloned.1.call-start = ((), (), s32[]{:S(2)}) async-start(), calls=%async_computation.17 | async-start | bytes 3932160 | tf_op jit(solution)/shard_map/all_gather | solution.py:203
  236.6 424.4 %copy-start.17 = (f32[1536]{0:T(1024)}, f32[1536]{0:T(1024)S(1)}, u32[]{:S(2)}) copy-start(f32[1536]{0:T(1024)S(1)} %convert_element_type.178) | copy-start | bytes 18436
  346.7 314.3 %copy-start.25 = (f32[256]{0:T(256)}, f32[256]{0:T(256)S(1)}, u32[]{:S(2)}) copy-start(f32[256]{0:T(256)S(1)} %get-tuple-element.753) | copy-start | bytes 3076
  346.7 314.3 %copy-start.29 = (f32[256]{0:T(256)}, f32[256]{0:T(256)S(1)}, u32[]{:S(2)}) copy-start(f32[256]{0:T(256)S(1)} %get-tuple-element.752) | copy-start | bytes 3076
  347.9 228.3 %all-gather.26.cloned.1.call-start = ((), (), s32[]{:S(2)}) async-start(), calls=%async_computation.19 | async-start | bytes 3538944 | tf_op jit(solution)/shard_map/all_gather | solution.py:182
  348.6 310.2 %reduce-scatter.16.cloned.1.call-start = ((), (), s32[]{:S(2)}) async-start(), calls=%async_computation.23 | async-start | bytes 3932160 | tf_op jit(solution)/shard_map/reduce_scatter | solution.py:249
  576.2 10.9 copy-start.35
  587.1 3.6 copy-start.36
  587.1 3.9 copy-start.37
  587.1 4.5 copy-start.39
  598.4 62.7 %copy-start.8 = (bf16[256,1536]{1,0:T(8,128)(2,1)S(1)}, bf16[256,1536]{1,0:T(8,128)(2,1)}, u32[]{:S(2)}) copy-start(bf16[256,1536]{1,0:T(8,128)(2,1)} %param.31) | copy-start | bytes 2359300
  598.4 128.9 %all-gather.32.cloned.1.call-start = ((), (), s32[]{:S(2)}) async-start(), calls=%async_computation.24 | async-start | bytes 3932160 | tf_op jit(solution)/shard_map/all_gather | solution.py:270
  661.0 71.2 %copy-start.31 = (f32[256]{0:T(256)}, f32[256]{0:T(256)S(1)}, u32[]{:S(2)}) copy-start(f32[256]{0:T(256)S(1)} %broadcast_multiply_fusion.1) | copy-start | bytes 3076
  663.6 201.8 %all-reduce.8.cloned.1.call-start = ((), (), s32[]{:S(2)}) async-start(), calls=%async_computation.29 | async-start | bytes 294912 | tf_op jit(solution)/shard_map/psum | solution.py:336
  733.7 95.0 %copy-start.16 = (f32[1024,6]{0,1:T(8,128)S(1)}, f32[1024,6]{0,1:T(8,128)}, u32[]{:S(2)}) copy-start(f32[1024,6]{0,1:T(8,128)} %copy-done.15) | copy-start | bytes 73732
  743.5 4.8 copy-start.1
  744.3 5.4 copy-start.23
  759.4 4.2 copy-start.1
  760.2 4.8 copy-start.23
  774.7 4.8 copy-start.1
  775.5 5.4 copy-start.23
  790.7 4.2 copy-start.1
  791.4 4.8 copy-start.23
  806.8 4.2 copy-start.23
  821.4 4.0 copy-start.23
  832.3 83.0 %reduce-scatter.30.cloned.1.call-start = ((), (), s32[]{:S(2)}) async-start(), calls=%async_computation.33 | async-start | bytes 3538944 | tf_op jit(solution)/shard_map/reduce_scatter | solution.py:262
  841.6 123.3 %reduce-scatter.28.cloned.1.call-start = ((), (), s32[]{:S(2)}) async-start(), calls=%async_computation.32 | async-start | bytes 3538944 | tf_op jit(solution)/shard_map/reduce_scatter | solution.py:259
  849.3 165.4 %reduce-scatter.32.cloned.1.call-start = ((), (), s32[]{:S(2)}) async-start(), calls=%async_computation.34 | async-start | bytes 3538944 | tf_op jit(solution)/shard_map/reduce_scatter | solution.py:265
  857.0 212.6 %all-reduce.10.cloned.1.call-start = ((), (), s32[]{:S(2)}) async-start(), calls=%async_computation.30 | async-start | bytes 294912 | tf_op jit(solution)/shard_map/psum | solution.py:336
  865.5 245.0 %reduce-scatter.26.cloned.1.call-start = ((), (), s32[]{:S(2)}) async-start(), calls=%async_computation.31 | async-start | bytes 1327104 | tf_op jit(solution)/shard_map/reduce_scatter | solution.py:321
  870.8 279.9 %reduce-scatter.20.cloned.1.call-start = ((), (), s32[]{:S(2)}) async-start(), calls=%async_computation.26 | async-start | bytes 1327104 | tf_op jit(solution)/shard_map/reduce_scatter | solution.py:312
  875.8 314.9 %reduce-scatter.22.cloned.1.call-start = ((), (), s32[]{:S(2)}) async-start(), calls=%async_computation.27 | async-start | bytes 1327104 | tf_op jit(solution)/shard_map/reduce_scatter | solution.py:315
  881.5 349.6 %reduce-scatter.24.cloned.1.call-start = ((), (), s32[]{:S(2)}) async-start(), calls=%async_computation.28 | async-start | bytes 1327104 | tf_op jit(solution)/shard_map/reduce_scatter | solution.py:318
  886.5 407.2 %reduce-scatter.18.cloned.1.call-start = ((), (), s32[]{:S(2)}) async-start(), calls=%async_computation.25 | async-start | bytes 3932160 | tf_op jit(solution)/shard_map/reduce_scatter | solution.py:295
  897.0 459.4 %reduce-scatter.14.cloned.1.call-start = ((), (), s32[]{:S(2)}) async-start(), calls=%async_computation.21 | async-start | bytes 3932160 | tf_op jit(solution)/shard_map/reduce_scatter | solution.py:209
  904.9 388.8 %copy-start.5 = (bf16[256,1536]{1,0:T(8,128)(2,1)S(1)}, bf16[256,1536]{1,0:T(8,128)(2,1)}, u32[]{:S(2)}) copy-start(bf16[256,1536]{1,0:T(8,128)(2,1)} %param.18) | copy-start | bytes 2359300
  904.9 388.8 %copy-start.20 = (f32[1536]{0:T(1024)S(1)}, f32[1536]{0:T(1024)}, u32[]{:S(2)}) copy-start(f32[1536]{0:T(1024)} %copy-done.19) | copy-start | bytes 18436
  904.9 388.8 %copy-start.28 = (f32[256]{0:T(256)S(1)}, f32[256]{0:T(256)}, u32[]{:S(2)}) copy-start(f32[256]{0:T(256)} %copy-done.27) | copy-start | bytes 3076
  917.3 378.0 %copy-start.24 = (f32[1536]{0:T(1024)S(1)}, f32[1536]{0:T(1024)}, u32[]{:S(2)}) copy-start(f32[1536]{0:T(1024)} %get-tuple-element.677) | copy-start | bytes 18436
  917.3 439.2 %copy-start.9 = (bf16[256,1536]{1,0:T(8,128)(2,1)S(1)}, bf16[256,1536]{1,0:T(8,128)(2,1)}, u32[]{:S(2)}) copy-start(bf16[256,1536]{1,0:T(8,128)(2,1)} %param.31) | copy-start | bytes 2359300
  917.3 439.2 %copy-start.18 = (f32[1536]{0:T(1024)S(1)}, f32[1536]{0:T(1024)}, u32[]{:S(2)}) copy-start(f32[1536]{0:T(1024)} %copy-done.17) | copy-start | bytes 18436
  917.3 439.2 %copy-start.26 = (f32[256]{0:T(256)S(1)}, f32[256]{0:T(256)}, u32[]{:S(2)}) copy-start(f32[256]{0:T(256)} %copy-done.25) | copy-start | bytes 3076
  917.3 439.2 %copy-start.30 = (f32[256]{0:T(256)S(1)}, f32[256]{0:T(256)}, u32[]{:S(2)}) copy-start(f32[256]{0:T(256)} %copy-done.29) | copy-start | bytes 3076
  917.3 439.2 %copy-start.32 = (f32[256]{0:T(256)S(1)}, f32[256]{0:T(256)}, u32[]{:S(2)}) copy-start(f32[256]{0:T(256)} %copy-done.31) | copy-start | bytes 3076
  917.3 439.2 %copy-start.33 = (f32[256]{0:T(256)S(1)}, f32[256]{0:T(256)}, u32[]{:S(2)}) copy-start(f32[256]{0:T(256)} %get-tuple-element.750) | copy-start | bytes 3076
  (25 other events, 49.7 us)
Sparse Core Ops, SparseCore 0:
  30.7 62.8 all-gather.11
  95.5 22.6 all-gather.17
  120.1 24.0 all-gather.15
  146.0 24.0 all-gather.13
  171.8 24.0 all-gather.19
  234.2 110.7 reduce-scatter.11
  346.6 64.0 all-gather.29
  412.5 30.9 all-gather.27
  445.4 32.3 all-gather.23
  479.8 63.4 all-gather.21
  545.2 30.9 all-gather.25
  598.5 60.2 reduce-scatter.15
  663.8 63.5 all-gather.31
  832.5 32.9 all-reduce.7
  869.1 46.2 reduce-scatter.29
  918.6 46.2 reduce-scatter.27
  968.5 46.1 reduce-scatter.31
  1017.7 51.9 all-reduce.9
  1072.8 37.5 reduce-scatter.25
  1113.9 36.7 reduce-scatter.19
  1153.9 36.7 reduce-scatter.21
  1194.3 36.7 reduce-scatter.23
  1233.4 60.2 reduce-scatter.17
  1295.8 60.5 reduce-scatter.13
